TPU v7x, 512 devices: a whole 4x4x16 slice. The times are simulated.
512 devices in a mesh: seq: 32 (over z, y_lo), mp: 16 (over x, y_hi, core).
Axes of the slice: x: 4, y: 4 (y_hi: 2, y_lo: 2; y = y_hi * 2 + y_lo), z: 16, core: 2. Of those that a mesh axis runs over, the one named last changes fastest.
Arguments:
- queries: bfloat16 [16384, 8192], P('seq', 'mp'), may hold values from -6 to 6
- keys_in: bfloat16 [16384, 8192], P('seq', 'mp'), may hold values from -6 to 6
- values_in: bfloat16 [16384, 8192], P('seq', 'mp'), may hold values from -6 to 6
- residual: bfloat16 [16384, 8192], P('seq', 'mp')
- short_taps: bfloat16 [3, 7, 8192], P(None, None, 'mp'), may hold values from -2 to 2
- mr_filter: bfloat16 [128, 512], P('seq', 'mp'), may hold values from -0.5 to 0.5
- norm_gain: bfloat16 [8192], P('mp'), may hold values from 0.5 to 1.5
- predecessor: int32 [32], replicated, may hold values from -1 to 31, as said below
- stretch_lengths: int32 [32], replicated, may hold values from 1 to 512, as said below
Outputs:
- mixed: bfloat16 [16384, 8192], P('seq', 'mp')
- normed: bfloat16 [16384, 8192], P('seq', 'mp')
Inputs may be any that keep to these rules, and one draw needn't show every extreme that they name: predecessor[j] is the stretch holding the preceding 512 tokens of stretch j's genome, or -1 for a genome's first stretch; each stretch precedes at most one stretch, and the chains have no cycles. `stretch_lengths`: every stretch that precedes another stretch is full (512 valid tokens); valid tokens come first.
All inputs are finite; a program needn't handle non-finite values.
Results may differ from a plain program's by a relative error of at most 0.0049.
Values may be sent and summed in bfloat16 or wider, within the bound.
A program may use at most 64 MiB of HBM per device.

v0:
```python
import jax
import jax.numpy as jnp
from jax import lax
from jax.sharding import PartitionSpec as P

EPSILON = 1e-06


def featurize(extended, taps):
    length = extended.shape[0] - 8
    total = jnp.zeros((length, extended.shape[1]), jnp.float32)
    for offset in range(taps.shape[0]):
        total = total + taps[offset].astype(jnp.float32) * extended[
            8 - offset : 8 - offset + length
        ].astype(jnp.float32)
    return total


def toeplitz_blocks(filter_rows):
    tap_count = filter_rows.shape[0]
    group_count = filter_rows.shape[1]
    flipped = filter_rows[::-1].T
    pattern = jnp.concatenate(
        [
            jnp.zeros((group_count, 1), filter_rows.dtype),
            flipped,
            jnp.zeros((group_count, tap_count), filter_rows.dtype),
        ],
        axis=1,
    )
    tiled = jnp.tile(pattern, (1, tap_count))[:, : 2 * tap_count * tap_count]
    return tiled.reshape(group_count, tap_count, 2 * tap_count)


def long_conv(extended, filter_rows, group_size):
    tap_count = filter_rows.shape[0]
    length = extended.shape[0] - tap_count
    blocks = length // tap_count
    channels = extended.shape[1]
    pieces = extended.reshape(blocks + 1, tap_count, channels)
    windows = jnp.concatenate([pieces[:-1], pieces[1:]], axis=1).reshape(
        blocks, 2 * tap_count, channels // group_size, group_size
    )
    matrices = toeplitz_blocks(filter_rows)
    result = jnp.einsum("gij,bjgc->bigc", matrices, windows, preferred_element_type=jnp.float32)
    return result.reshape(length, channels)


def body(
    queries,
    keys_in,
    values_in,
    residual,
    short_taps,
    mr_filter,
    norm_gain,
    predecessor,
    stretch_lengths,
):
    row_count, width = queries.shape
    device = lax.axis_index("seq")
    filter_rows = lax.all_gather(mr_filter, "seq", axis=0, tiled=True)
    tap_count = filter_rows.shape[0]
    group_size = width // filter_rows.shape[1]
    blank = jnp.zeros((8, width), queries.dtype)
    key_feat = featurize(jnp.concatenate([blank, keys_in]), short_taps[1])
    value_feat = featurize(jnp.concatenate([blank, values_in]), short_taps[2])
    mixed_in = (key_feat * value_feat).astype(jnp.bfloat16)
    state_tail = mixed_in[row_count - tap_count :][None]
    raw_tail = jnp.concatenate(
        [queries[row_count - 8 :], keys_in[row_count - 8 :], values_in[row_count - 8 :]], axis=1
    )[None]
    source = predecessor[device]
    carry = (jnp.zeros_like(state_tail), jnp.zeros_like(raw_tail))
    piece = (
        lax.all_gather(state_tail, "seq", axis=0, tiled=True),
        lax.all_gather(raw_tail, "seq", axis=0, tiled=True),
    )
    count = piece[0].shape[0]
    inside = (source >= 0) & (source < count)
    offset = jnp.clip(source, 0, count - 1)
    prev_state, prev_raw = tuple(
        (
            jnp.where(inside, lax.dynamic_slice_in_dim(member, offset, 1, 0), kept)
            for member, kept in zip(piece, carry)
        )
    )
    prev_rows = prev_raw[0]
    prev_query = prev_rows[:, :width]
    prev_key = prev_rows[:, width : 2 * width]
    prev_value = prev_rows[:, 2 * width :]
    query_feat = featurize(jnp.concatenate([prev_query, queries]), short_taps[0])
    head_key = featurize(jnp.concatenate([prev_key, keys_in[:8]]), short_taps[1])
    head_value = featurize(jnp.concatenate([prev_value, values_in[:8]]), short_taps[2])
    head_mixed = (head_key * head_value).astype(jnp.bfloat16)
    mixed_in = jnp.concatenate([head_mixed, mixed_in[8:]])
    extended = jnp.concatenate([prev_state[0], mixed_in])
    filtered = long_conv(extended, filter_rows, group_size)
    valid = (jnp.arange(row_count, dtype=jnp.int32) < stretch_lengths[device])[:, None]
    mixed = jnp.where(valid, query_feat * filtered, 0.0).astype(jnp.bfloat16)
    summed = residual.astype(jnp.float32) + mixed.astype(jnp.float32)
    squares_total = lax.psum(jnp.sum(summed * summed, axis=1), "mp")
    scale_rows = lax.rsqrt(squares_total / (width * lax.axis_size("mp")) + EPSILON)
    normed = jnp.where(
        valid, summed * scale_rows[:, None] * norm_gain.astype(jnp.float32), 0.0
    ).astype(jnp.bfloat16)
    return (mixed, normed)


def solution(mesh):
    in_specs = (
        P("seq", "mp"),
        P("seq", "mp"),
        P("seq", "mp"),
        P("seq", "mp"),
        P(None, None, "mp"),
        P("seq", "mp"),
        P("mp"),
        P(),
        P(),
    )
    out_specs = (P("seq", "mp"), P("seq", "mp"))
    return jax.shard_map(body, mesh=mesh, in_specs=in_specs, out_specs=out_specs, check_vma=False)
```

profile of v0, /device:TPU:1, one launch (start us, length us, event | category | flops | bytes accessed | tf_op | source)
XLA Modules:
  0.0 226.0 jit_solution(18346637916515088260)
XLA Ops:
  7.2 0.0 copy-start.3
  7.2 0.0 all-gather.5.cloned.1.call-start
  7.2 1.0 slice_convert_fusion.20
  8.2 0.0 copy-start.4
  8.2 0.8 slice_convert_fusion.1
  9.0 5.3 %multiply_convert_fusion = bf16[512,512]{1,0:T(8,128)(2,1)S(1)} fusion(bf16[512,512]{1,0:T(8,128)(2,1)} %param.11, bf16[512,512]{1,0:T(8,128)(2,1)} %param.10, f32[512]{0:T(512)S(1)} %bitcast.92, f32[512]{0:T(512)S(1)} %bitcast.90, f32[512]{0:T(512)S(1)} %bitcast.66, f32[512]{0:T(512)S(1)} %bitcast.68, f32[512]{0:T(512)S(1)} %bitcast.70, ...), kind=kLoop, calls=%fused_computation.17 | loop fusion | flops 11010048 | bytes 1601536 | tf_op jit(solution)/shard_map/convert_element_type | solution.py:68
  14.4 0.0 copy-start
  14.4 0.7 slice.328
  15.1 0.0 all-gather.5.cloned.1.call-update
  15.2 0.6 dynamic_slice.13
  16.9 1.0 copy.66
  18.5 0.0 copy-done.4
  18.5 56.7 %all-gather.2 = bf16[32,4,32]{2,1,0:T(4,128)(2,1)S(1)} all-gather(bf16[1,4,32]{2,1,0:T(4,128)(2,1)S(1)} %bitcast.102), channel_id=1, replica_groups=mesh['seq'=32,'mp'=16] {'seq'}, dimensions={0}, use_global_device_ids=true | all-gather | bytes 8448 | tf_op jit(solution)/shard_map/all_gather | solution.py:62
  75.2 0.1 copy.73
  75.3 0.1 rev.3
  75.4 0.1 pad.4.clone
  75.5 0.1 maximum_maximum_fusion
  75.6 0.3 tile.4
  75.8 4.4 %tile.10 = bf16[32,32896]{1,0:T(8,128)(2,1)} reshape(bf16[32,128,257]{2,1,0:T(8,128)(2,1)S(1)} %tile.4) | data formatting | bytes 4210688 | tf_op jit(solution)/shard_map/tile | solution.py:31
  80.3 1.6 slice-done
  81.9 0.5 copy.79
  82.4 0.0 copy-start.5
  82.4 0.0 slice-start.1
  82.4 0.8 fusion.27
  83.2 59.5 %all-gather = bf16[256,1536]{1,0:T(8,128)(2,1)S(1)} all-gather(bf16[8,1536]{1,0:T(8,128)(2,1)S(1)} %pad_maximum_fusion.4), channel_id=2, replica_groups=mesh['seq'=32,'mp'=16] {'seq'}, dimensions={0}, use_global_device_ids=true | all-gather | bytes 811008 | tf_op jit(solution)/shard_map/all_gather | solution.py:77
  142.8 0.2 copy.67
  143.0 0.0 copy-done.7
  143.0 0.7 dynamic_slice.12
  143.6 1.3 copy.75
  144.9 0.7 iota_compare_fusion
  145.6 0.1 multiply_convert_fusion.1
  145.7 4.9 %all-gather.5.cloned.1.call-done = bf16[4096,512]{1,0:T(8,128)(2,1)} async-done(((bf16[128,512]{1,0:T(8,128)(2,1)}), bf16[4096,512]{1,0:T(8,128)(2,1)}) %all-gather.5.cloned.1.call-update) | async-done | bytes 4194320 | tf_op jit(solution)/shard_map/all_gather | solution.py:76
  150.6 0.9 select_bitcast_fusion
  151.5 1.0 pad_maximum_fusion
  152.6 2.1 copy.69
  154.7 2.0 concatenate.42
  156.7 1.9 copy.71
  158.6 1.0 copy.70
  159.6 1.2 concatenate.44
  160.8 0.1 copy.72
  160.9 1.9 fusion.2
  162.8 0.4 copy.74
  163.2 0.6 copy-done.2
  163.8 2.1 multiply_reduce_fusion
  165.9 51.0 %psum.7 = f32[512]{0:T(512)S(1)} all-reduce(f32[512]{0:T(512)S(1)} %get-tuple-element.8), channel_id=1, replica_groups=mesh['seq'=32,'mp'=16] {'mp'}, use_global_device_ids=true, to_apply=%region_1.2 | all-reduce | flops 512 | bytes 4096 | tf_op jit(solution)/shard_map/psum | solution.py:102
  216.9 1.0 copy.76
  217.9 0.2 select_convert_fusion
  218.1 1.0 copy.77
  (20 shorter events, 0.1 us)
Async XLA Ops:
  7.2 8.0 %copy-start.6 = (s32[32]{0:T(128)S(1)}, s32[32]{0:T(128)}, u32[]{:S(2)}) copy-start(s32[32]{0:T(128)} %param.16) | copy-start | bytes 388
  7.2 9.7 %copy-start.3 = (bf16[512,512]{1,0:T(8,128)(2,1)S(1)}, bf16[512,512]{1,0:T(8,128)(2,1)}, u32[]{:S(2)}) copy-start(bf16[512,512]{1,0:T(8,128)(2,1)} %param.9) | copy-start | bytes 1572868
  7.2 143.4 %all-gather.5.cloned.1.call-start = ((), (), s32[]{:S(2)}) async-start(), calls=%async_computation | async-start | bytes 4325376 | tf_op jit(solution)/shard_map/all_gather | solution.py:76
  8.2 10.2 %copy-start.4 = (bf16[4,32]{1,0:T(4,128)(2,1)S(1)}, bf16[4,32]{1,0:T(4,128)(2,1)}, u32[]{:S(2)}) copy-start(bf16[4,32]{1,0:T(4,128)(2,1)} %param.14) | copy-start | bytes 772
  14.4 61.1 %copy-start = (bf16[512,512]{1,0:T(8,128)(2,1)}, bf16[512,512]{1,0:T(8,128)(2,1)S(1)}, u32[]{:S(2)}) copy-start(bf16[512,512]{1,0:T(8,128)(2,1)S(1)} %multiply_convert_fusion) | copy-start | bytes 1572868
  80.3 1.6 slice-start
  81.9 1.3 slice-start.2
  81.9 61.1 %copy-start.7 = (s32[32]{0:T(128)S(1)}, s32[32]{0:T(128)}, u32[]{:S(2)}) copy-start(s32[32]{0:T(128)} %param.17) | copy-start | bytes 388
  82.4 62.5 %copy-start.5 = (bf16[512]{0:T(512)(128)(2,1)S(1)}, bf16[512]{0:T(512)(128)(2,1)}, u32[]{:S(2)}) copy-start(bf16[512]{0:T(512)(128)(2,1)} %param.15) | copy-start | bytes 3076
  82.4 69.1 %slice-start.1 = ((bf16[512,512]{1,0:T(8,128)(2,1)}), bf16[504,512]{1,0:T(8,128)(2,1)S(1)}, s32[]{:S(2)}) async-start(bf16[512,512]{1,0:T(8,128)(2,1)} %copy-done), calls=%async_computation.2 | async-start | bytes 1032192 | tf_op jit(solution)/shard_map/slice | solution.py:96
  152.6 6.0 %copy-start.1 = (bf16[512,512]{1,0:T(8,128)(2,1)S(1)}, bf16[512,512]{1,0:T(8,128)(2,1)}, u32[]{:S(2)}) copy-start(bf16[512,512]{1,0:T(8,128)(2,1)} %get-tuple-element.11) | copy-start | bytes 1572868
  162.8 1.0 copy-start.2
Sparse Core Ops, SparseCore 0:
  15.3 135.2 all-gather.4
where the time goes:
time: 227 us; the launch traced here: 226 us
  blocking collectives  167 us (74%)
  local copies, waits for them, and re-layouts  23.7 us (10%)
  between operations  16 us (7%)
  other arithmetic  12.3 us (5%)
  waiting for transfers between devices  4.95 us (2%)
    all_gather x1, blocking collectives, body(): lax.all_gather(raw_tail, 'seq', axis=0, tiled=True)  59.5 us
    all_gather x1, blocking collectives, body(): filter_rows = lax.all_gather(mr_filter, 'seq', axis=0, tiled=True)  56.7 us
    psum x1, blocking collectives, body(): squares_total = lax.psum(jnp.sum(summed * summed, axis=1), 'mp')  51 us
    unnamed x22, local copies, waits for them, and re-layouts  5.46 us
    convert_element_type x1, other arithmetic, body(): mixed_in = (key_feat * value_feat).astype(jnp.bfloat16)  5.34 us
    concatenate x4, local copies, waits for them, and re-layouts, long_conv(): jnp.concatenate([pieces[:-1], pieces[1:]], axis=1)  5.16 us
    all_gather x1, waiting for transfers between devices, body(): lax.all_gather(state_tail, 'seq', axis=0, tiled=True)  4.93 us
    another operation x2, local copies, waits for them, and re-layouts, toeplitz_blocks(): tiled = jnp.tile(pattern, (1, tap_count))[:, :2 * tap_count * tap_count]  4.73 us
  transfers between devices with their start and end apart: 1, of which 1 were waited for; matrix products, arithmetic and copies ran while one was open for 5% of the time, Pallas kernels for 0%

commit v1 on v0

--- a/solution.py
+++ b/solution.py
@@ -99,7 +99,7 @@
     valid = (jnp.arange(row_count, dtype=jnp.int32) < stretch_lengths[device])[:, None]
     mixed = jnp.where(valid, query_feat * filtered, 0.0).astype(jnp.bfloat16)
     summed = residual.astype(jnp.float32) + mixed.astype(jnp.float32)
-    squares_total = lax.psum(jnp.sum(summed * summed, axis=1), "mp")
+    squares_total = jnp.sum(lax.all_gather(jnp.sum(summed * summed, axis=1), "mp"), axis=0)
     scale_rows = lax.rsqrt(squares_total / (width * lax.axis_size("mp")) + EPSILON)
     normed = jnp.where(
         valid, summed * scale_rows[:, None] * norm_gain.astype(jnp.float32), 0.0

time: 227 us -> 218 us (0.960)
  blocking collectives: 167 us -> 159 us
    psum x1 -> x0, blocking collectives: 51 us -> none  [body(): squares_total = lax.psum(jnp.sum(summed * summed, axis=1), 'mp')]
    all_gather x0 -> x1, blocking collectives: none -> 42.5 us  [body(): lax.all_gather(jnp.sum(summed * summed, axis=1), 'mp')]
where the time goes in v1:
time: 218 us
  blocking collectives  159 us (73%)
  local copies, waits for them, and re-layouts  23.7 us (11%)
  between operations  16 us (7%)
  other arithmetic  12.3 us (6%)
  waiting for transfers between devices  4.95 us (2%)
    all_gather x1, blocking collectives, body(): lax.all_gather(raw_tail, 'seq', axis=0, tiled=True)  59.5 us
    all_gather x1, blocking collectives, body(): filter_rows = lax.all_gather(mr_filter, 'seq', axis=0, tiled=True)  56.7 us
    all_gather x1, blocking collectives, body(): lax.all_gather(jnp.sum(summed * summed, axis=1), 'mp')  42.5 us
    unnamed x22, local copies, waits for them, and re-layouts  5.46 us
    convert_element_type x1, other arithmetic, body(): mixed_in = (key_feat * value_feat).astype(jnp.bfloat16)  5.34 us
    concatenate x4, local copies, waits for them, and re-layouts, long_conv(): jnp.concatenate([pieces[:-1], pieces[1:]], axis=1)  5.16 us
    all_gather x1, waiting for transfers between devices, body(): lax.all_gather(state_tail, 'seq', axis=0, tiled=True)  4.93 us
    another operation x2, local copies, waits for them, and re-layouts, toeplitz_blocks(): tiled = jnp.tile(pattern, (1, tap_count))[:, :2 * tap_count * tap_count]  4.73 us
  transfers between devices with their start and end apart: 1, of which 1 were waited for; matrix products, arithmetic and copies ran while one was open for 5% of the time, Pallas kernels for 0%

profile of v1, /device:TPU:1, one launch (start us, length us, event | category | flops | bytes accessed | tf_op | source)
XLA Modules:
  0.0 217.6 jit_solution(11321914940495258178)
XLA Ops:
  7.2 0.0 copy-start.3
  7.2 0.0 all-gather.7.cloned.1.call-start
  7.2 1.0 slice_convert_fusion.20
  8.2 0.0 copy-start.4
  8.2 0.8 slice_convert_fusion.1
  9.0 5.3 %multiply_convert_fusion = bf16[512,512]{1,0:T(8,128)(2,1)S(1)} fusion(bf16[512,512]{1,0:T(8,128)(2,1)} %param.11, bf16[512,512]{1,0:T(8,128)(2,1)} %param.10, f32[512]{0:T(512)S(1)} %bitcast.93, f32[512]{0:T(512)S(1)} %bitcast.91, f32[512]{0:T(512)S(1)} %bitcast.67, f32[512]{0:T(512)S(1)} %bitcast.69, f32[512]{0:T(512)S(1)} %bitcast.71, ...), kind=kLoop, calls=%fused_computation.17 | loop fusion | flops 11010048 | bytes 1601536 | tf_op jit(solution)/shard_map/convert_element_type | solution.py:68
  14.4 0.0 copy-start
  14.4 0.7 slice.328
  15.1 0.0 all-gather.7.cloned.1.call-update
  15.2 0.6 dynamic_slice.13
  16.9 1.0 copy.66
  18.5 0.0 copy-done.4
  18.5 56.7 %all-gather.3 = bf16[32,4,32]{2,1,0:T(4,128)(2,1)S(1)} all-gather(bf16[1,4,32]{2,1,0:T(4,128)(2,1)S(1)} %bitcast.104), channel_id=1, replica_groups=mesh['seq'=32,'mp'=16] {'seq'}, dimensions={0}, use_global_device_ids=true | all-gather | bytes 8448 | tf_op jit(solution)/shard_map/all_gather | solution.py:62
  75.2 0.1 copy.73
  75.3 0.1 rev.3
  75.4 0.1 pad.4.clone
  75.5 0.1 maximum_maximum_fusion
  75.6 0.3 tile.4
  75.8 4.4 %tile.10 = bf16[32,32896]{1,0:T(8,128)(2,1)} reshape(bf16[32,128,257]{2,1,0:T(8,128)(2,1)S(1)} %tile.4) | data formatting | bytes 4210688 | tf_op jit(solution)/shard_map/tile | solution.py:31
  80.3 1.6 slice-done
  81.9 0.5 copy.79
  82.4 0.0 copy-start.5
  82.4 0.0 slice-start.1
  82.4 0.8 fusion.27
  83.2 59.5 %all-gather = bf16[256,1536]{1,0:T(8,128)(2,1)S(1)} all-gather(bf16[8,1536]{1,0:T(8,128)(2,1)S(1)} %pad_maximum_fusion.4), channel_id=2, replica_groups=mesh['seq'=32,'mp'=16] {'seq'}, dimensions={0}, use_global_device_ids=true | all-gather | bytes 811008 | tf_op jit(solution)/shard_map/all_gather | solution.py:77
  142.8 0.2 copy.67
  143.0 0.0 copy-done.7
  143.0 0.7 dynamic_slice.12
  143.6 1.3 copy.75
  144.9 0.7 iota_compare_fusion
  145.6 0.1 multiply_convert_fusion.1
  145.7 4.9 %all-gather.7.cloned.1.call-done = bf16[4096,512]{1,0:T(8,128)(2,1)} async-done(((bf16[128,512]{1,0:T(8,128)(2,1)}), bf16[4096,512]{1,0:T(8,128)(2,1)}) %all-gather.7.cloned.1.call-update) | async-done | bytes 4194320 | tf_op jit(solution)/shard_map/all_gather | solution.py:76
  150.6 0.9 select_bitcast_fusion
  151.5 1.0 pad_maximum_fusion
  152.6 2.1 copy.69
  154.7 2.0 concatenate.42
  156.7 1.9 copy.71
  158.6 1.0 copy.70
  159.6 1.2 concatenate.44
  160.8 0.1 copy.72
  160.9 1.9 fusion.2
  162.8 0.4 copy.74
  163.2 0.6 copy-done.2
  163.8 2.1 multiply_reduce_fusion
  165.9 42.5 %all-gather.4 = f32[16,1,512]{2,1,0:T(1,128)S(1)} all-gather(f32[1,1,512]{2,1,0:T(1,128)S(1)} %bitcast.102), channel_id=4, replica_groups=mesh['seq'=32,'mp'=16] {'mp'}, dimensions={0}, use_global_device_ids=true | all-gather | bytes 34816 | tf_op jit(solution)/shard_map/all_gather | solution.py:102
  208.5 1.0 copy.76
  209.5 0.2 select_convert_fusion
  209.7 1.0 copy.77
  (21 shorter events, 0.1 us)
Async XLA Ops:
  7.2 8.0 %copy-start.6 = (s32[32]{0:T(128)S(1)}, s32[32]{0:T(128)}, u32[]{:S(2)}) copy-start(s32[32]{0:T(128)} %param.16) | copy-start | bytes 388
  7.2 9.7 %copy-start.3 = (bf16[512,512]{1,0:T(8,128)(2,1)S(1)}, bf16[512,512]{1,0:T(8,128)(2,1)}, u32[]{:S(2)}) copy-start(bf16[512,512]{1,0:T(8,128)(2,1)} %param.9) | copy-start | bytes 1572868
  7.2 143.4 %all-gather.7.cloned.1.call-start = ((), (), s32[]{:S(2)}) async-start(), calls=%async_computation | async-start | bytes 4325376 | tf_op jit(solution)/shard_map/all_gather | solution.py:76
  8.2 10.2 %copy-start.4 = (bf16[4,32]{1,0:T(4,128)(2,1)S(1)}, bf16[4,32]{1,0:T(4,128)(2,1)}, u32[]{:S(2)}) copy-start(bf16[4,32]{1,0:T(4,128)(2,1)} %param.14) | copy-start | bytes 772
  14.4 61.1 %copy-start = (bf16[512,512]{1,0:T(8,128)(2,1)}, bf16[512,512]{1,0:T(8,128)(2,1)S(1)}, u32[]{:S(2)}) copy-start(bf16[512,512]{1,0:T(8,128)(2,1)S(1)} %multiply_convert_fusion) | copy-start | bytes 1572868
  80.3 1.6 slice-start
  81.9 1.3 slice-start.2
  81.9 61.1 %copy-start.7 = (s32[32]{0:T(128)S(1)}, s32[32]{0:T(128)}, u32[]{:S(2)}) copy-start(s32[32]{0:T(128)} %param.17) | copy-start | bytes 388
  82.4 62.5 %copy-start.5 = (bf16[512]{0:T(512)(128)(2,1)S(1)}, bf16[512]{0:T(512)(128)(2,1)}, u32[]{:S(2)}) copy-start(bf16[512]{0:T(512)(128)(2,1)} %param.15) | copy-start | bytes 3076
  82.4 69.1 %slice-start.1 = ((bf16[512,512]{1,0:T(8,128)(2,1)}), bf16[504,512]{1,0:T(8,128)(2,1)S(1)}, s32[]{:S(2)}) async-start(bf16[512,512]{1,0:T(8,128)(2,1)} %copy-done), calls=%async_computation.2 | async-start | bytes 1032192 | tf_op jit(solution)/shard_map/slice | solution.py:96
  152.6 6.0 %copy-start.1 = (bf16[512,512]{1,0:T(8,128)(2,1)S(1)}, bf16[512,512]{1,0:T(8,128)(2,1)}, u32[]{:S(2)}) copy-start(bf16[512,512]{1,0:T(8,128)(2,1)} %get-tuple-element.11) | copy-start | bytes 1572868
  162.8 1.0 copy-start.2
Sparse Core Ops, SparseCore 0:
  15.3 135.2 all-gather.6
